TPU v7x, 32 devices: a whole 2x2x4 slice. The times are simulated.
32 devices in a mesh: row: 8 (over z, y), col: 4 (over x, core).
Axes of the slice: x: 2, y: 2, z: 4, core: 2. Of those that a mesh axis runs over, the one named last changes fastest.
Arguments:
- a_weights: bfloat16 [4096, 1024], P('row', 'col'), may hold values from 0.0001 to 1, as said below
- tile_mask: int32 [8, 2], replicated, may hold values from 0 to 1, as said below
- pair_mask: int32 [8, 8], replicated, may hold values from 0 to 1, as said below
Outputs:
- jaccard: bfloat16 [4096, 4096], P('row', 'col')
Inputs may be any that keep to these rules, and one draw needn't show every extreme that they name: `a_weights`: all weights positive. `tile_mask`: 1 where a tile is present; tile (I, I mod 2) of every block row I is present. `pair_mask`: symmetric, with ones on the diagonal.
All inputs are finite; a program needn't handle non-finite values.
Results may differ from a plain program's by a relative error of at most 0.001.
Values may be sent and summed in bfloat16 or wider, within the bound.
A program may use at most 64 MiB of HBM per device.

v0:
```python
import jax
import jax.numpy as jnp
from jax import lax
from jax.sharding import PartitionSpec as P

BLOCK = 512


def broadcast(value, axis, source):
    kept = jnp.where(lax.axis_index(axis) == source, value, 0).astype(value.dtype)
    return lax.psum(kept, axis)


def expand_tiles(flags):
    return jnp.repeat(jnp.repeat(flags, BLOCK, axis=0), BLOCK, axis=1)


def body(a_weights, tile_mask, pair_mask):
    row_index = lax.axis_index("row")
    col_index = lax.axis_index("col")
    pair_count = lax.axis_size("row") // lax.axis_size("col")
    blocks_here = a_weights.shape[0] // BLOCK
    own_flags = lax.dynamic_slice_in_dim(tile_mask, row_index * blocks_here, blocks_here, 0)
    own_mask = expand_tiles(own_flags).astype(jnp.bfloat16)
    gathered = lax.all_gather(a_weights, "col", axis=1, tiled=True)
    own_panel = gathered * own_mask
    row_degree = jnp.einsum("ik,ik->i", own_panel, own_panel, preferred_element_type=jnp.float32)
    remotes = [
        broadcast(own_panel, "row", pair_count * col_index + offset) for offset in range(pair_count)
    ]
    outputs = []
    for offset in range(pair_count):
        col_first = (pair_count * col_index + offset) * blocks_here
        remote = remotes[offset]
        pair_tiles = lax.dynamic_slice(
            pair_mask, (row_index * blocks_here, col_first), (blocks_here, blocks_here)
        )
        pair_open = expand_tiles(pair_tiles) > 0
        col_degree = jnp.einsum("ik,ik->i", remote, remote, preferred_element_type=jnp.float32)
        shared = lax.dot_general(
            own_panel, remote, (((1,), (1,)), ((), ())), preferred_element_type=jnp.float32
        )
        weights = shared / (row_degree[:, None] + col_degree[None, :] - shared)
        outputs.append(jnp.where(pair_open, weights, jnp.zeros_like(weights)))
    return jnp.concatenate(outputs, axis=1).astype(jnp.bfloat16)


def solution(mesh):
    in_specs = (P("row", "col"), P(), P())
    out_specs = P("row", "col")
    return jax.shard_map(body, mesh=mesh, in_specs=in_specs, out_specs=out_specs, check_vma=False)
```

profile of v0, /device:TPU:0, one launch (start us, length us, event | category | flops | bytes accessed | tf_op | source)
XLA Modules:
  0.0 146.8 jit_solution(6093091236768662315)
XLA Ops:
  6.5 0.0 all-gather.2.cloned.1.call-start
  6.5 0.7 all-gather.2.cloned.1.call-update
  7.3 0.0 all-reduce.3.cloned.1.call-start
  7.3 0.9 fusion.17
  8.2 0.1 broadcast_bitcast_fusion
  8.3 20.2 %all-gather.2.cloned.1.call-done = bf16[512,1024]{1,0:T(8,128)(2,1)} async-done(((bf16[512,256]{1,0:T(8,128)(2,1)}), bf16[512,1024]{1,0:T(8,128)(2,1)}) %all-gather.2.cloned.1.call-update) | async-done | bytes 1048592 | tf_op jit(solution)/shard_map/all_gather | solution.py:25
  28.5 2.7 %broadcast_select_fusion.1 = (bf16[512,1024]{1,0:T(8,128)(2,1)}, bf16[512,1024]{1,0:T(8,128)(2,1)}) fusion(pred[]{:T(512)S(6)} %eq.6, bf16[512,1024]{1,0:T(8,128)(2,1)} %all-gather.2.cloned.1.call-done, bf16[1024]{0:T(1024)(128)(2,1)S(1)} %bitcast.7, pred[]{:T(512)S(6)} %eq.7), kind=kLoop, calls=%fused_computation.14 | loop fusion | flops 1572864 | bytes 3147778 | tf_op jit(solution)/shard_map/jit(_where)/select_n | solution.py:10
  31.2 0.0 copy-start
  31.2 0.0 all-reduce.3.cloned.1.call-update
  31.2 1.5 fusion.18
  34.0 0.0 copy-done
  34.0 0.3 fusion.2
  34.3 100.0 %all-reduce.3.cloned.1.call-done = (bf16[512,1024]{1,0:T(8,128)(2,1)}, bf16[512,1024]{1,0:T(8,128)(2,1)}) async-done(((bf16[512,1024]{1,0:T(8,128)(2,1)}, bf16[512,1024]{1,0:T(8,128)(2,1)}), (bf16[512,1024]{1,0:T(8,128)(2,1)}, bf16[512,1024]{1,0:T(8,128)(2,1)})) %all-reduce.3.cloned.1.call-update) | async-done | bytes 2097168 | tf_op jit(solution)/shard_map/psum | solution.py:11
  134.4 0.0 copy-start.2
  134.4 2.1 %fusion = (f32[512]{0:T(512)S(1)}, f32[512]{0:T(512)S(1)}) fusion(bf16[512,1024]{1,0:T(8,128)(2,1)} %get-tuple-element.5, bf16[512,1024]{1,0:T(8,128)(2,1)} %get-tuple-element.6), kind=kLoop, calls=%fused_computation.1 | loop fusion | flops 3144704 | bytes 2101248 | tf_op jit(solution)/shard_map/ik,ik->i/dot_general | solution.py:39
  136.5 0.0 copy-done.2
  136.5 0.0 copy-start.1
  136.5 0.8 fusion.4
  137.3 0.4 copy-done.1
  137.7 0.8 fusion.6
  138.5 0.1 pad_maximum_fusion
  138.6 1.3 copy.4
  (1 shorter events, 0.0 us)
Async XLA Ops:
  6.5 21.9 %all-gather.2.cloned.1.call-start = ((), (), s32[]{:S(2)}) async-start(), calls=%async_computation | async-start | bytes 1310720 | tf_op jit(solution)/shard_map/all_gather | solution.py:25
  7.3 127.1 %all-reduce.3.cloned.1.call-start = ((), (), s32[]{:S(2)}) async-start(), calls=%async_computation.1 | async-start | bytes 4194304 | tf_op jit(solution)/shard_map/psum | solution.py:11
  31.2 2.8 %copy-start = (bf16[512,1024]{1,0:T(8,128)(2,1)S(1)}, bf16[512,1024]{1,0:T(8,128)(2,1)}, u32[]{:S(2)}) copy-start(bf16[512,1024]{1,0:T(8,128)(2,1)} %all-gather.2.cloned.1.call-done) | copy-start | bytes 3145732
  134.4 2.1 %copy-start.2 = (bf16[512,1024]{1,0:T(8,128)(2,1)S(1)}, bf16[512,1024]{1,0:T(8,128)(2,1)}, u32[]{:S(2)}) copy-start(bf16[512,1024]{1,0:T(8,128)(2,1)} %get-tuple-element.6) | copy-start | bytes 3145732
  136.5 1.2 copy-start.1
Sparse Core Ops, SparseCore 0:
  8.9 19.5 all-gather.1
  32.1 102.1 all-reduce.2
where the time goes:
time: 147 us
  waiting for transfers between devices  121 us (82%)
  between operations  14.8 us (10%)
  other arithmetic  6.09 us (4%)
  local copies, waits for them, and re-layouts  3.28 us (2%)
  matrix products  1.58 us (1%)
    psum x1, waiting for transfers between devices, broadcast(): return lax.psum(kept, axis)  100 us
    all_gather x1, waiting for transfers between devices, body(): gathered = lax.all_gather(a_weights, 'col', axis=1, tiled=True)  20.2 us
  transfers between devices with their start and end apart: 2, of which 2 were waited for; matrix products, arithmetic and copies ran while one was open for 2% of the time, Pallas kernels for 0%

commit v1 on v0

--- a/solution.py
+++ b/solution.py
@@ -4,6 +4,16 @@
 from jax.sharding import PartitionSpec as P
 
 BLOCK = 512
+
+
+def pass_along(shard, axis, dim):
+    peers = lax.axis_size(axis)
+    held, parts = (shard, [shard])
+    for _ in range(peers - 1):
+        held = lax.ppermute(held, axis, [(i, (i + 1) % peers) for i in range(peers)])
+        parts.insert(0, held)
+    line = jnp.concatenate(parts, axis=dim)
+    return jnp.roll(line, (lax.axis_index(axis) + 1) * shard.shape[dim], axis=dim)
 
 
 def broadcast(value, axis, source):
@@ -22,7 +32,7 @@
     blocks_here = a_weights.shape[0] // BLOCK
     own_flags = lax.dynamic_slice_in_dim(tile_mask, row_index * blocks_here, blocks_here, 0)
     own_mask = expand_tiles(own_flags).astype(jnp.bfloat16)
-    gathered = lax.all_gather(a_weights, "col", axis=1, tiled=True)
+    gathered = pass_along(a_weights, "col", 1)
     own_panel = gathered * own_mask
     row_degree = jnp.einsum("ik,ik->i", own_panel, own_panel, preferred_element_type=jnp.float32)
     remotes = [

time: 147 us -> 145 us (0.986)
  waiting for transfers between devices: 121 us -> 118 us
    all_gather x1 -> x0, waiting for transfers between devices: 20.2 us -> none  [body(): gathered = lax.all_gather(a_weights, 'col', axis=1, tiled=True)]
    ppermute x0 -> x3, waiting for transfers between devices: none -> 16.9 us  [pass_along(): lax.ppermute(held, axis, [(i, (i + 1) % peers) for i in range(peers)])]
  transfers between devices with their start and end apart: 2 -> 4, of which waited for: 2 -> 4; matrix products, arithmetic and copies ran while one was open for 2% -> 2% of each run, Pallas kernels for 0% -> 0%
where the time goes in v1:
time: 145 us
  waiting for transfers between devices  118 us (81%)
  between operations  14.8 us (10%)
  other arithmetic  5.22 us (4%)
  local copies, waits for them, and re-layouts  4.42 us (3%)
  matrix products  1.62 us (1%)
    psum x1, waiting for transfers between devices, broadcast(): return lax.psum(kept, axis)  101 us
    ppermute x3, waiting for transfers between devices, pass_along(): lax.ppermute(held, axis, [(i, (i + 1) % peers) for i in range(peers)])  16.9 us
  transfers between devices with their start and end apart: 4, of which 4 were waited for; matrix products, arithmetic and copies ran while one was open for 2% of the time, Pallas kernels for 0%

profile of v1, /device:TPU:0, one launch (start us, length us, event | category | flops | bytes accessed | tf_op | source)
XLA Modules:
  0.0 144.6 jit_solution(1626656254750767912)
XLA Ops:
  6.5 0.0 all-reduce.3.cloned.1.call-start
  6.5 0.5 collective-permute-start
  7.0 6.3 %collective-permute-done = bf16[512,256]{1,0:T(8,128)(2,1)S(1)} collective-permute-done((bf16[512,256]{1,0:T(8,128)(2,1)}, bf16[512,256]{1,0:T(8,128)(2,1)S(1)}, u32[]{:S(2)}, u32[]{:S(2)}) %collective-permute-start) | collective-permute-done | bytes 262176 | tf_op jit(solution)/shard_map/ppermute | solution.py:13
  13.3 0.0 collective-permute-start.1
  13.3 5.8 %collective-permute-done.1 = bf16[512,256]{1,0:T(8,128)(2,1)S(1)} collective-permute-done((bf16[512,256]{1,0:T(8,128)(2,1)S(1)}, bf16[512,256]{1,0:T(8,128)(2,1)S(1)}, u32[]{:S(2)}, u32[]{:S(2)}) %collective-permute-start.1) | collective-permute-done | bytes 262176 | tf_op jit(solution)/shard_map/ppermute | solution.py:13
  19.0 0.0 collective-permute-start.2
  19.1 0.9 fusion.9
  19.9 0.1 broadcast_bitcast_fusion
  20.0 4.8 %collective-permute-done.2 = bf16[512,256]{1,0:T(8,128)(2,1)S(1)} collective-permute-done((bf16[512,256]{1,0:T(8,128)(2,1)S(1)}, bf16[512,256]{1,0:T(8,128)(2,1)S(1)}, u32[]{:S(2)}, u32[]{:S(2)}) %collective-permute-start.2) | collective-permute-done | bytes 262176 | tf_op jit(solution)/shard_map/ppermute | solution.py:13
  24.9 1.0 constant_dynamic-update-slice_fusion.4
  26.0 0.0 copy-done.2
  26.1 1.8 %broadcast_select_fusion.1 = (bf16[512,1024]{1,0:T(8,128)(2,1)}, bf16[512,1024]{1,0:T(8,128)(2,1)}) fusion(pred[]{:T(512)S(6)} %eq.9, bf16[1024]{0:T(1024)(128)(2,1)S(1)} %bitcast.7, bf16[512,2048]{1,0:T(8,128)(2,1)S(1)} %constant_dynamic-update-slice_fusion, s32[]{:T(128)S(6)} %select_n.48, pred[]{:T(512)S(6)} %eq.10), kind=kLoop, calls=%fused_computation.15 | loop fusion | flops 3145728 | bytes 3147782 | tf_op jit(solution)/shard_map/jit(_where)/select_n | solution.py:20
  27.9 0.0 all-reduce.3.cloned.1.call-update
  27.9 1.4 fusion.12
  30.6 0.4 fusion.2
  31.0 101.2 %all-reduce.3.cloned.1.call-done = (bf16[512,1024]{1,0:T(8,128)(2,1)}, bf16[512,1024]{1,0:T(8,128)(2,1)}) async-done(((bf16[512,1024]{1,0:T(8,128)(2,1)}, bf16[512,1024]{1,0:T(8,128)(2,1)}), (bf16[512,1024]{1,0:T(8,128)(2,1)}, bf16[512,1024]{1,0:T(8,128)(2,1)})) %all-reduce.3.cloned.1.call-update) | async-done | bytes 2097168 | tf_op jit(solution)/shard_map/psum | solution.py:21
  132.2 2.1 %fusion = (f32[512]{0:T(512)S(1)}, f32[512]{0:T(512)S(1)}) fusion(bf16[512,1024]{1,0:T(8,128)(2,1)} %get-tuple-element.5, bf16[512,1024]{1,0:T(8,128)(2,1)} %get-tuple-element.6), kind=kLoop, calls=%fused_computation.1 | loop fusion | flops 3144704 | bytes 2101248 | tf_op jit(solution)/shard_map/ik,ik->i/dot_general | solution.py:49
  134.3 0.0 copy-done.1
  134.3 0.0 copy-start
  134.3 0.8 fusion.4
  135.1 0.4 copy-done
  135.5 0.8 fusion.6
  136.4 0.1 pad_maximum_fusion
  136.4 1.3 copy.4
  (10 shorter events, 0.2 us)
Async XLA Ops:
  6.5 19.5 %copy-start.2 = (bf16[512,256]{1,0:T(8,128)(2,1)S(1)}, bf16[512,256]{1,0:T(8,128)(2,1)}, u32[]{:S(2)}) copy-start(bf16[512,256]{1,0:T(8,128)(2,1)} %param.3) | copy-start | bytes 786436
  6.5 125.7 %all-reduce.3.cloned.1.call-start = ((), (), s32[]{:S(2)}) async-start(), calls=%async_computation | async-start | bytes 4194304 | tf_op jit(solution)/shard_map/psum | solution.py:21
  6.5 6.7 %collective-permute-start = (bf16[512,256]{1,0:T(8,128)(2,1)}, bf16[512,256]{1,0:T(8,128)(2,1)S(1)}, u32[]{:S(2)}, u32[]{:S(2)}) collective-permute-start(bf16[512,256]{1,0:T(8,128)(2,1)} %param.3), channel_id=1, source_target_pairs={{0,1},{1,2},{2,3},{3,0},{4,5},{5,6},{6,7},{7,4},{8,9},{9,10},{10,1... | collective-permute-start | bytes 786440 | tf_op jit(solution)/shard_map/ppermute | solution.py:13
  13.3 5.8 %collective-permute-start.1 = (bf16[512,256]{1,0:T(8,128)(2,1)S(1)}, bf16[512,256]{1,0:T(8,128)(2,1)S(1)}, u32[]{:S(2)}, u32[]{:S(2)}) collective-permute-start(bf16[512,256]{1,0:T(8,128)(2,1)S(1)} %collective-permute-done), channel_id=1, source_target_pairs={{0,1},{1,2},{2,3},{3,0},{4,5},{5,6},{6,7},{7,4},{8,9},{9,10},{10,1... | collective-permute-start | bytes 786440 | tf_op jit(solution)/shard_map/ppermute | solution.py:13
  19.0 5.8 %collective-permute-start.2 = (bf16[512,256]{1,0:T(8,128)(2,1)S(1)}, bf16[512,256]{1,0:T(8,128)(2,1)S(1)}, u32[]{:S(2)}, u32[]{:S(2)}) collective-permute-start(bf16[512,256]{1,0:T(8,128)(2,1)S(1)} %collective-permute-done.1), channel_id=1, source_target_pairs={{0,1},{1,2},{2,3},{3,0},{4,5},{5,6},{6,7},{7,4},{8,9},{9,10},{10,1... | collective-permute-start | bytes 786440 | tf_op jit(solution)/shard_map/ppermute | solution.py:13
  132.2 2.1 %copy-start.1 = (bf16[512,1024]{1,0:T(8,128)(2,1)S(1)}, bf16[512,1024]{1,0:T(8,128)(2,1)}, u32[]{:S(2)}) copy-start(bf16[512,1024]{1,0:T(8,128)(2,1)} %get-tuple-element.6) | copy-start | bytes 3145732
  134.3 1.2 copy-start
Sparse Core Ops, SparseCore 0:
  28.1 104.0 all-reduce.2
